TPU v7x, 128 devices: a whole 4x4x4 slice. The times are simulated.
128 devices in a mesh: seq: 32 (over y, x, core), head: 4 (over z), dp: 1.
Axes of the slice: x: 4, y: 4, z: 4, core: 2. Of those that a mesh axis runs over, the one named last changes fastest.
Arguments:
- token_ids: int32 [8192], P(('dp', 'seq')), may hold values from 0 to 8191, as said below
- token_tables: bfloat16 [2, 256, 8192], P(None, 'head'), may hold values from -12 to 1, as said below
- ssm_input: bfloat16 [8192, 16384], P(('dp', 'seq'), 'head'), may hold values from -6 to 6
- ssm_gate: bfloat16 [8192, 16384], P(('dp', 'seq'), 'head'), may hold values from -6 to 6
- ssm_bc: bfloat16 [8192, 2, 2048], P(('dp', 'seq'), None, 'head'), may hold values from -6 to 6
- conv_input: bfloat16 [4, 16384], P(None, 'head'), may hold values from -3 to 3
- conv_bc: bfloat16 [4, 2, 2048], P(None, None, 'head'), may hold values from -3 to 3
- skip_gain: float32 [256], P('head'), may hold values from 0.5 to 1.5
- norm_gain: bfloat16 [16384], P('head'), may hold values from 0.25 to 1.75
- queries: bfloat16 [8192, 8192], P(('dp', 'seq'), 'head'), may hold values from -24 to 24
- keys_values: bfloat16 [8192, 2, 1024], P(('dp', 'seq'), None, 'head'), may hold values from -9 to 9
Outputs:
- mamba_out: bfloat16 [8192, 16384], P(('dp', 'seq'), 'head')
- attn_out: bfloat16 [8192, 8192], P(('dp', 'seq'), 'head')
Inputs may be any that keep to these rules, and one draw needn't show every extreme that they name: `token_ids`: token ids into the tables. `token_tables`: slice 0 holds positive decay rates.
All inputs are finite; a program needn't handle non-finite values.
Results may differ from a plain program's by a relative error of at most 0.0065.
Values may be sent and summed in bfloat16 or wider, within the bound.
No kernel may reach another device: no remote copies, remote signals or barrier semaphores. Data moves between devices by JAX's collectives and lax.ppermute only.
A program may use at most 384 MiB of HBM per device.

v0:
```python
import jax
import jax.numpy as jnp
from jax import lax
from jax.sharding import PartitionSpec as P

MHDIM = 64
STATE = 256
CONV = 4
QHEADS = 64
KVHEADS = 8
HDIM = 128
SPAN = 128


EPSILON = 1e-05
HIGHEST = lax.Precision.HIGHEST


def from_behind(value, axis, steps):
    count = lax.axis_size(axis)
    first, last = (max(0, -steps), min(count, count - steps))
    return lax.ppermute(value, axis, [(source, source + steps) for source in range(first, last)])


def carried_in(x, axis, join, neutral):
    place = lax.axis_index(axis)
    gathered = jax.tree.map(
        lambda a, kind: lax.all_gather(a.astype(kind), axis), x, (jnp.bfloat16, jnp.bfloat16)
    )
    state = jax.tree.map(lambda a, e: jnp.zeros_like(a) + jnp.asarray(e, a.dtype), x, neutral)

    def one(lap, state):
        return join(
            state,
            jax.tree.map(
                lambda a, own: lax.dynamic_index_in_dim(a, lap, 0, False).astype(own.dtype),
                gathered,
                x,
            ),
        )

    return lax.fori_loop(0, place, one, state)


def conv_front(front, values, weight):
    tap_count = weight.shape[0]
    length = values.shape[0]
    padded = jnp.concatenate([front, values], 0)
    summed = jnp.zeros(values.shape, jnp.float32)
    for offset in range(tap_count):
        summed = summed + weight[offset].astype(jnp.float32) * padded[
            offset : offset + length
        ].astype(jnp.float32)
    return jax.nn.silu(summed).astype(jnp.bfloat16)


def join_states(earlier, later):
    return (earlier[0] + later[0], jnp.exp(later[0])[..., None, None] * earlier[1] + later[1])


def make_absorb(query_grid, query_places):
    kv_local = query_grid.shape[1]
    factor = HDIM ** (-0.5)

    def absorb(carry, block, key_start):
        running_top, running_sum, running_acc = carry
        block_rows = block.shape[0]
        key_block = block[:, 0].reshape(block_rows, kv_local, HDIM)
        value_block = block[:, 1].reshape(block_rows, kv_local, HDIM)
        scores = (
            jnp.einsum("tkjd,skd->kjts", query_grid, key_block, preferred_element_type=jnp.float32)
            * factor
        )
        key_places = key_start + jnp.arange(block_rows, dtype=jnp.int32)
        visible = query_places[:, None] >= key_places[None, :]
        scores = jnp.where(visible, scores, -jnp.inf)
        new_top = jnp.maximum(running_top, jnp.max(scores, axis=3))
        shrink = jnp.exp(running_top - new_top)
        expo = jnp.exp(scores - new_top[..., None])
        new_sum = running_sum * shrink + jnp.sum(expo, axis=3)
        new_acc = running_acc * shrink[..., None] + jnp.einsum(
            "kjts,skd->kjtd",
            expo.astype(jnp.bfloat16),
            value_block,
            preferred_element_type=jnp.float32,
        )
        return (new_top, new_sum, new_acc)

    return absorb


def start_carry(kv_local, per_kv, rows):
    return (
        jnp.full((kv_local, per_kv, rows), -1e30, jnp.float32),
        jnp.zeros((kv_local, per_kv, rows), jnp.float32),
        jnp.zeros((kv_local, per_kv, rows, HDIM), jnp.float32),
    )


def finish(carry):
    attended = carry[2] / carry[1][..., None]
    rows = attended.shape[2]
    return attended.transpose(2, 0, 1, 3).reshape(rows, -1).astype(jnp.bfloat16)


def local(
    token_ids,
    token_tables,
    ssm_input,
    ssm_gate,
    ssm_bc,
    conv_input,
    conv_bc,
    skip_gain,
    norm_gain,
    queries,
    keys_values,
):
    token_rows = ssm_input.shape[0]
    head_count = token_tables.shape[1]
    group_count = ssm_bc.shape[2] // STATE
    per_group = head_count // group_count
    block_count = token_rows // SPAN
    edge_rows = CONV - 1
    front_input, front_bc = from_behind(
        (ssm_input[token_rows - edge_rows :], ssm_bc[token_rows - edge_rows :]), "seq", 1
    )
    x_conv = conv_front(front_input, ssm_input, conv_input)
    bc_conv = conv_front(front_bc, ssm_bc, conv_bc)
    rate_values = jnp.take(token_tables[0], token_ids, axis=1).astype(jnp.float32)
    steps = jax.nn.softplus(jnp.take(token_tables[1], token_ids, axis=1).astype(jnp.float32))
    log_decay = (
        (-rate_values).reshape(group_count, per_group, block_count, SPAN).transpose(2, 0, 1, 3)
    )
    step_size = steps.reshape(group_count, per_group, block_count, SPAN).transpose(2, 0, 1, 3)
    cumulative = jnp.cumsum(log_decay, axis=3)
    x_blocks = x_conv.reshape(block_count, SPAN, group_count, per_group, MHDIM)
    b_blocks = bc_conv[:, 0].reshape(block_count, SPAN, group_count, STATE)
    c_blocks = bc_conv[:, 1].reshape(block_count, SPAN, group_count, STATE)
    places = jnp.arange(SPAN, dtype=jnp.int32)
    causal = places[:, None] >= places[None, :]
    gram_matrix = jnp.einsum(
        "btgn,bsgn->bgts", c_blocks, b_blocks, preferred_element_type=jnp.float32
    )
    decays = jnp.exp(
        jnp.where(causal, cumulative[..., :, None] - cumulative[..., None, :], -jnp.inf)
    )
    weights = (gram_matrix[:, :, None] * decays * step_size[..., None, :]).astype(jnp.bfloat16)
    inside = jnp.einsum("bgrts,bsgrp->btgrp", weights, x_blocks, preferred_element_type=jnp.float32)
    last_log = cumulative[..., -1]
    tail_weight = jnp.exp(last_log[..., None] - cumulative) * step_size
    x_float = x_blocks.astype(jnp.float32)
    scaled_input = x_float * tail_weight.transpose(0, 3, 1, 2)[..., None]
    deltas = jnp.einsum(
        "bsgrp,bsgn->bgrpn", scaled_input, b_blocks.astype(jnp.float32), precision=HIGHEST
    )

    def advance(state, item):
        block_log, block_delta = item
        return (jnp.exp(block_log)[..., None, None] * state + block_delta, state)

    zero_state = jnp.zeros((group_count, per_group, MHDIM, STATE), jnp.float32)
    local_final, local_enter = lax.scan(advance, zero_state, (last_log, deltas))
    device_log = jnp.sum(last_log, axis=0)
    zero_log = jnp.zeros_like(device_log)
    incoming = carried_in((device_log, local_final), "seq", join_states, (zero_log, zero_state))[1]
    block_before = jnp.cumsum(last_log, axis=0) - last_log
    entering = local_enter + jnp.exp(block_before)[..., None, None] * incoming[None]
    carried = jnp.exp(cumulative).transpose(0, 3, 1, 2)[..., None] * jnp.einsum(
        "btgn,bgrpn->btgrp", c_blocks.astype(jnp.float32), entering, precision=HIGHEST
    )
    skip_weight = skip_gain.reshape(group_count, per_group)
    mixed = inside + carried + skip_weight[:, :, None] * x_float
    gate_act = jax.nn.silu(ssm_gate.astype(jnp.float32)).reshape(
        token_rows, group_count, per_group * MHDIM
    )
    gated = mixed.reshape(token_rows, group_count, per_group * MHDIM) * gate_act
    inverse_rms = lax.rsqrt(jnp.mean(gated * gated, axis=2, keepdims=True) + EPSILON)
    mamba_out = (
        (gated * inverse_rms).reshape(token_rows, head_count * MHDIM)
        * norm_gain.astype(jnp.float32)
    ).astype(jnp.bfloat16)
    kv_local = keys_values.shape[2] // HDIM
    per_kv = QHEADS // KVHEADS
    own_shard = lax.axis_index("seq")
    query_grid = queries.reshape(token_rows, kv_local, per_kv, HDIM)
    query_places = own_shard * token_rows + jnp.arange(token_rows, dtype=jnp.int32)
    absorb = make_absorb(query_grid, query_places)
    piece = lax.all_gather(keys_values, "seq", axis=0, tiled=True)
    block_rows = min(piece.shape[0], token_rows)
    shard_count = piece.shape[0] // block_rows
    shards = piece.reshape(shard_count, block_rows, 2, piece.shape[2])

    def one_shard(inner, shard_index):
        return (absorb(inner, shards[shard_index], shard_index * block_rows), None)

    result, _ = lax.scan(
        one_shard,
        start_carry(kv_local, per_kv, token_rows),
        jnp.arange(shard_count, dtype=jnp.int32),
    )
    attn_out = finish(result)
    return (mamba_out, attn_out)


def solution(mesh):
    in_specs = (
        P(("dp", "seq")),
        P(None, "head", None),
        P(("dp", "seq"), "head"),
        P(("dp", "seq"), "head"),
        P(("dp", "seq"), None, "head"),
        P(None, "head"),
        P(None, None, "head"),
        P("head"),
        P("head"),
        P(("dp", "seq"), "head"),
        P(("dp", "seq"), None, "head"),
    )
    out_specs = (P(("dp", "seq"), "head"), P(("dp", "seq"), "head"))
    return jax.shard_map(local, mesh=mesh, in_specs=in_specs, out_specs=out_specs, check_vma=False)
```

profile of v0, /device:TPU:95, one launch (start us, length us, event | category | flops | bytes accessed | tf_op | source)
XLA Modules:
  0.0 864.1 jit_solution(5748057286722885103)
XLA Ops:
  36.0 7.7 multiply_convert_fusion.2
  46.3 5.6 fusion.21
  51.9 18.8 %while.41 = (s32[]{:T(128)}, f32[2,32,64,256]{3,2,1,0:T(8,128)}, f32[2,2,32,64,256]{4,3,2,1,0:T(8,128)}, f32[2,2,32]{2,1,0:T(2,128)S(1)}, f32[2,2,32,64,256]{4,3,2,1,0:T(8,128)}, /*index=5*/s32[]{:T(128)}, s32[]{:T(128)}) while((s32[]{:T(128)}, f32[2,32,64,256]{3,2,1,0:T(8,128)}, f32[2,2,32,64,256]{4,3,2,1,0:T(8,128)}, ...), condition=%wide.region_2.4_spmd.clone, body=%wide.region_1.3_spmd.clone.sunk | while | flops 4194307 | bytes 54527352 | solution.py:163
  59.6 5.1 bitcast_dynamic-update-slice_fusion.2
  65.9 4.7 bitcast_add_fusion.2
  70.7 3.9 convert_element_type.129
  75.2 4.1 copy.118
  79.3 4.7 convert_multiply_fusion
  84.0 5.8 reshape.111
  94.2 23.8 %all-gather.2 = bf16[32,2,32]{2,1,0:T(2,128)(2,1)} all-gather(bf16[1,2,32]{2,1,0:T(2,128)(2,1)S(1)} %bitcast.159), channel_id=2, replica_groups=mesh['seq'=32,'head'=4,'dp'=1] {'seq'}, dimensions={0}, use_global_device_ids=true | all-gather | bytes 4224 | tf_op jit(solution)/shard_map/all_gather | solution.py:28
  123.4 516.2 %while.42 = (s32[]{:T(128)}, f32[2,8,256]{2,1,0:T(8,128)S(1)}, f32[2,8,256]{2,1,0:T(8,128)}, f32[2,8,256,128]{3,2,1,0:T(8,128)S(1)}, s32[32]{0:T(128)}, /*index=...) while((s32[]{:T(128)}, f32[2,8,256]{2,1,0:T(8,128)S(1)}, ...), condition=%wide.region_11.13_spmd.clone, body=%wide.region_8.12_spmd.clone.sunk | while | flops 550064640 | bytes 37097752 | solution.py:197
  150.3 3.8 fusion.79
  163.4 3.7 fusion.78
  183.1 4.1 fusion.79
  196.5 3.7 fusion.78
  229.5 3.7 fusion.78
  262.4 3.8 fusion.78
  278.5 3.7 fusion.78
  310.5 3.7 fusion.78
  342.5 3.7 fusion.78
  374.5 3.7 fusion.78
  406.5 3.7 fusion.78
  438.5 3.7 fusion.78
  470.6 3.7 fusion.78
  502.6 3.7 fusion.78
  534.6 3.7 fusion.78
  566.6 3.7 fusion.78
  598.6 3.7 fusion.78
  630.6 3.7 fusion.78
  645.4 185.1 %while.40 = (s32[]{:T(128)}, f32[2,32,64,256]{3,2,1,0:T(8,128)}, s32[]{:T(128)}, bf16[32,2,32]{2,1,0:T(2,128)(2,1)}, bf16[32,2,32,64,256]{4,3,2,1,0:T(8,128)(2,1)}, /*index=5*/s32[]{:T(128)}, s32[]{:T(128)}, s32[]{:T(128)}) while((s32[]{:T(128)}, f32[2,32,64,256]{3,2,1,0:T(8,128)}, s32[]{:T(128)}, bf16[32,2,32]{2,1,0:T(2,128)(2,1)}, ...), condition=%wide.region_6.8_spmd, body=%wide.region_5.7_spmd.sunk | while | flops 3145797 | bytes 10486527 | solution.py:42
  646.2 5.3 convert_add_fusion.2
  652.2 5.3 convert_add_fusion.2
  658.2 5.3 convert_add_fusion.2
  664.2 5.3 convert_add_fusion.2
  670.2 5.3 convert_add_fusion.2
  676.1 5.3 convert_add_fusion.2
  682.1 5.3 convert_add_fusion.2
  688.0 5.3 convert_add_fusion.2
  694.0 5.3 convert_add_fusion.2
  700.0 5.3 convert_add_fusion.2
  706.0 5.3 convert_add_fusion.2
  712.0 5.3 convert_add_fusion.2
  718.0 5.3 convert_add_fusion.2
  723.9 5.3 convert_add_fusion.2
  729.9 5.3 convert_add_fusion.2
  735.9 5.3 convert_add_fusion.2
  741.8 5.3 convert_add_fusion.2
  747.7 5.3 convert_add_fusion.2
  753.7 5.3 convert_add_fusion.2
  759.6 5.3 convert_add_fusion.2
  765.6 5.3 convert_add_fusion.2
  771.6 5.3 convert_add_fusion.2
  777.6 5.3 convert_add_fusion.2
  783.6 5.3 convert_add_fusion.2
  789.5 5.3 convert_add_fusion.2
  795.4 5.3 convert_add_fusion.2
  801.4 5.3 convert_add_fusion.2
  807.3 5.3 convert_add_fusion.2
  813.3 5.3 convert_add_fusion.2
  819.3 5.3 convert_add_fusion.2
  825.3 5.3 convert_add_fusion.2
  830.7 11.0 %fusion.17 = f32[2,2,32,64,128]{4,3,2,1,0:T(8,128)} fusion(f32[2,2,32,64,256]{4,3,2,1,0:T(8,128)} %get-tuple-element.118, f32[2,32,64,256]{3,2,1,0:T(8,128)} %get-tuple-element.120, f32[2,2,32]{2,1,0:T(2,128)S(1)} %copy-done.24, bf16[2,128,2,256,1]{3,2,1,0,4:T(2,128)(2,1)S(1)} %bitcast.149), kind=kOutput, calls=%fused_computation.30 | convolution fusion | flops 3225419776 | bytes 17039872 | tf_op jit(solution)/shard_map/btgn,bgrpn->btgrp/dot_general | solution.py:169
  841.7 7.2 fusion.31
  849.0 3.9 copy.117
  (715 shorter events, 454.1 us)
Async XLA Ops:
  7.2 10.0 %copy-start.28 = (s32[256]{0:T(256)S(1)}, s32[256]{0:T(256)}, u32[]{:S(2)}) copy-start(s32[256]{0:T(256)} %param.19) | copy-start | bytes 3076
  7.2 115.6 %all-gather.6.cloned.1.call-start = ((), (), s32[]{:S(2)}) async-start(), calls=%async_computation | async-start | bytes 8650752 | tf_op jit(solution)/shard_map/all_gather | solution.py:189
  8.9 634.0 %all-gather.8.cloned.1.call-start = ((), (), s32[]{:S(2)}) async-start(), calls=%async_computation.1 | async-start | bytes 69206016 | tf_op jit(solution)/shard_map/all_gather | solution.py:28
  9.7 19.2 %collective-permute-start.1 = (bf16[3,2,512]{2,1,0:T(2,128)(2,1)S(1)}, bf16[3,2,512]{2,1,0:T(2,128)(2,1)S(1)}, u32[]{:S(2)}, u32[]{:S(2)}) collective-permute-start(bf16[3,2,512]{2,1,0:T(2,128)(2,1)S(1)} %slice.78), channel_id=1, source_target_pairs={{0,4},{4,8},{8,12},{12,16},{16,20},{20,24},{24,28},{28,32},{32,36}... | collective-permute-start | bytes 18440 | tf_op jit(solution)/shard_map/ppermute | solution.py:22
  12.4 22.2 %collective-permute-start = (bf16[3,4096]{1,0:T(4,128)(2,1)}, bf16[3,4096]{1,0:T(4,128)(2,1)}, u32[]{:S(2)}, u32[]{:S(2)}) collective-permute-start(bf16[3,4096]{1,0:T(4,128)(2,1)} %slice.70), channel_id=1, source_target_pairs={{0,4},{4,8},{8,12},{12,16},{16,20},{20,24},{24,28},{28,32},{32,36}... | collective-permute-start | bytes 73736 | tf_op jit(solution)/shard_map/ppermute | solution.py:22
  15.4 9.5 %copy-start.17 = (bf16[4,4096]{1,0:T(4,128)(2,1)S(1)}, bf16[4,4096]{1,0:T(4,128)(2,1)}, u32[]{:S(2)}) copy-start(bf16[4,4096]{1,0:T(4,128)(2,1)} %param.24) | copy-start | bytes 98308
  15.4 10.1 %copy-start.25 = (bf16[4,2,512]{2,1,0:T(2,128)(2,1)S(1)}, bf16[4,2,512]{2,1,0:T(2,128)(2,1)}, u32[]{:S(2)}) copy-start(bf16[4,2,512]{2,1,0:T(2,128)(2,1)} %param.25) | copy-start | bytes 24580
  21.9 7.0 copy-start.9
  23.4 95.8 %copy-start.10 = (f32[2,2,32,128]{3,2,1,0:T(8,128)}, f32[2,2,32,128]{3,2,1,0:T(8,128)S(1)}, u32[]{:S(2)}) copy-start(f32[2,2,32,128]{3,2,1,0:T(8,128)S(1)} %reduce_window_sum.22) | copy-start | bytes 196612
  34.7 11.6 %copy-start.8 = (bf16[2,128,2,256]{3,2,1,0:T(2,128)(2,1)}, bf16[2,128,2,256]{3,2,1,0:T(2,128)(2,1)S(1)}, u32[]{:S(2)}) copy-start(bf16[2,128,2,256]{3,2,1,0:T(2,128)(2,1)S(1)} %reshape_squeeze.7) | copy-start | bytes 786436
  46.2 5.7 copy-start.3
  51.9 5.1 copy-start.1
  59.6 6.3 copy-start.1
  84.0 5.9 copy-start.29
  84.0 6.5 copy-start.26
  84.0 7.1 copy-start.12
  89.8 4.3 copy-start.27
  89.8 28.7 %copy-start.19 = (f32[2,2,32]{2,1,0:T(2,128)S(1)}, f32[2,2,32]{2,1,0:T(2,128)}, u32[]{:S(2)}) copy-start(f32[2,2,32]{2,1,0:T(2,128)} %copy-done.18) | copy-start | bytes 1540
  130.5 6.9 copy-start.13
  146.5 7.5 copy-start.13
  150.2 4.3 copy-start
  163.3 6.9 copy-start.13
  179.4 7.8 copy-start.13
  183.1 4.5 copy-start
  196.5 7.0 copy-start.13
  212.5 7.3 copy-start.13
  216.3 4.4 copy-start
  229.5 7.0 copy-start.13
  245.7 6.9 copy-start.13
  249.4 4.1 copy-start
  262.4 7.0 copy-start.13
  278.5 6.9 copy-start.13
  294.5 6.9 copy-start.13
  310.5 6.9 copy-start.13
  326.5 6.9 copy-start.13
  342.5 6.9 copy-start.13
  358.5 6.9 copy-start.13
  374.5 6.9 copy-start.13
  390.5 6.9 copy-start.13
  406.5 6.9 copy-start.13
  422.5 6.9 copy-start.13
  438.5 6.9 copy-start.13
  454.5 6.9 copy-start.13
  470.6 6.9 copy-start.13
  486.6 6.9 copy-start.13
  502.6 6.9 copy-start.13
  518.6 6.9 copy-start.13
  534.6 6.9 copy-start.13
  550.6 6.9 copy-start.13
  566.6 6.9 copy-start.13
  582.6 6.9 copy-start.13
  598.6 6.9 copy-start.13
  614.6 6.9 copy-start.13
  630.6 6.9 copy-start.13
  645.4 185.2 %copy-start.7 = (bf16[2,128,2,256]{3,2,1,0:T(2,128)(2,1)S(1)}, bf16[2,128,2,256]{3,2,1,0:T(2,128)(2,1)}, u32[]{:S(2)}) copy-start(bf16[2,128,2,256]{3,2,1,0:T(2,128)(2,1)} %copy-done.6) | copy-start | bytes 786436
  645.4 185.2 %copy-start.24 = (f32[2,2,32]{2,1,0:T(2,128)S(1)}, f32[2,2,32]{2,1,0:T(2,128)}, u32[]{:S(2)}) copy-start(f32[2,2,32]{2,1,0:T(2,128)} %fusion.45) | copy-start | bytes 1540
  830.6 11.1 %copy-start.4 = (bf16[2,128,2,32,64]{1,0,4,3,2:T(2,128)(2,1)S(1)}, bf16[2,128,2,32,64]{1,0,4,3,2:T(2,128)(2,1)}, u32[]{:S(2)}) copy-start(bf16[2,128,2,32,64]{1,0,4,3,2:T(2,128)(2,1)} %copy-done.3) | copy-start | bytes 6291460
  830.6 11.1 %copy-start.5 = (f32[2,128,2,32,64]{1,0,4,3,2:T(2,128)S(1)}, f32[2,128,2,32,64]{1,0,4,3,2:T(2,128)}, u32[]{:S(2)}) copy-start(f32[2,128,2,32,64]{1,0,4,3,2:T(2,128)} %reshape.111) | copy-start | bytes 12582916
  830.6 11.1 %copy-start.11 = (f32[2,2,32,128]{3,2,1,0:T(8,128)S(1)}, f32[2,2,32,128]{3,2,1,0:T(8,128)}, u32[]{:S(2)}) copy-start(f32[2,2,32,128]{3,2,1,0:T(8,128)} %copy-done.10) | copy-start | bytes 196612
  830.6 11.1 %copy-start.16 = (f32[2,2,128,128]{3,2,1,0:T(8,128)S(1)}, f32[2,2,128,128]{3,2,1,0:T(8,128)}, u32[]{:S(2)}) copy-start(f32[2,2,128,128]{3,2,1,0:T(8,128)} %fusion.50) | copy-start | bytes 786436
  830.6 11.1 %copy-start.21 = (f32[2,2,32,128]{3,2,1,0:T(8,128)S(1)}, f32[2,2,32,128]{3,2,1,0:T(8,128)}, u32[]{:S(2)}) copy-start(f32[2,2,32,128]{3,2,1,0:T(8,128)} %copy.111) | copy-start | bytes 196612
  830.6 11.1 %copy-start.22 = (f32[2,128,2,32]{1,3,2,0:T(8,128)S(1)}, f32[2,128,2,32]{1,3,2,0:T(8,128)}, u32[]{:S(2)}) copy-start(f32[2,128,2,32]{1,3,2,0:T(8,128)} %exponential_bitcast_fusion.2) | copy-start | bytes 196612
  830.7 11.1 %copy-start.23 = (pred[128,128]{1,0:T(8,128)(4,1)S(1)}, pred[128,128]{1,0:T(8,128)(4,1)}, u32[]{:S(2)}) copy-start(pred[128,128]{1,0:T(8,128)(4,1)} %iota_compare_fusion) | copy-start | bytes 49156
  830.7 11.1 %copy-start.30 = (f32[2,32]{1,0:T(2,128)S(1)}, f32[2,32]{1,0:T(2,128)}, u32[]{:S(2)}) copy-start(f32[2,32]{1,0:T(2,128)} %mul.293) | copy-start | bytes 772
  (65 other events, 177.3 us)
Sparse Core Ops, SparseCore 0:
  10.3 52.6 all-gather.5
  74.7 203.2 all-gather.7
where the time goes:
time: 870 us; the launch traced here: 864 us
  other arithmetic  336 us (39%)
  local copies, waits for them, and re-layouts  212 us (24%)
  matrix products  200 us (23%)
  loops' own time  75.2 us (9%)
  blocking collectives  23.8 us (3%)
  between operations  14.5 us (2%)
    add x31, other arithmetic, join_states(): jnp.exp(later[0])[..., None, None] * earlier[1] + later[1]  165 us
    dot_general x32, matrix products, absorb(): jnp.einsum('tkjd,skd->kjts', query_grid, key_block, preferred_element_typ...  119 us
    reduce_sum x32, other arithmetic, absorb(): new_sum = running_sum * shrink + jnp.sum(expo, axis=3)  104 us
    dynamic_slice x64, local copies, waits for them, and re-layouts, one_shard(): return (absorb(inner, shards[shard_index], shard_index * block_rows), None)  88.3 us
    another operation x1, loops' own time, local(): lax.scan(one_shard, start_carry(kv_local, per_kv, token_rows), jnp.arange...  75.1 us
    dot_general x32, matrix products, absorb(): jnp.einsum('kjts,skd->kjtd', expo.astype(jnp.bfloat16), value_block, pref...  55 us
    dynamic_slice x32, local copies, waits for them, and re-layouts, local(): lax.scan(one_shard, start_carry(kv_local, per_kv, token_rows), jnp.arange...  40.2 us
    all_gather x1, blocking collectives, carried_in(): lax.all_gather(a.astype(kind), axis)  23.8 us
  transfers between devices with their start and end apart: 4, of which 0 were waited for; matrix products, arithmetic and copies ran while one was open for 60% of the time, Pallas kernels for 0%

commit v1 on v0

v1 whole, which is shorter than its diff:
```python
import math

import jax
import jax.numpy as jnp
from jax import lax
from jax.experimental import pallas as pl
from jax.experimental.pallas import tpu as pltpu
from jax.sharding import PartitionSpec as P

MHDIM = 64
STATE = 256
CONV = 4
HDIM = 128
EPSILON = 1e-05
LOG2E = math.log2(math.e)
F32 = jnp.float32
BF16 = jnp.bfloat16

NY, NX, NCORE = 4, 4, 2
CHIPS = NY * NX
ROWS = 256
GROUP_CHANNELS = 2048
PAIRS = 16
EXTRA = 16
SROWS = STATE + EXTRA
MIB = 1 << 20


def params(mib=16):
    return pltpu.CompilerParams(vmem_limit_bytes=mib * MIB)


def cost(flops, nbytes, trans=0):
    return pl.CostEstimate(flops=int(flops), bytes_accessed=int(nbytes), transcendentals=int(trans))


def silu(v):
    half = 0.5 * v
    return half + half * jnp.tanh(half)


def split_hi_lo(v):
    hi = v.astype(BF16)
    lo = (v - hi.astype(F32)).astype(BF16)
    return hi, lo


def table_kernel(ids_ref, tab_ref, row_ref, col_ref, acc):
    step = pl.program_id(0)
    width = tab_ref.shape[2]

    @pl.when(step == 0)
    def _():
        acc[...] = jnp.zeros_like(acc)

    part = 1024
    for i in range(width // part):
        places = lax.broadcasted_iota(jnp.int32, (part, ROWS), 0) + (step * width + i * part)
        hot = jnp.where(places == ids_ref[...], 1.0, 0.0).astype(BF16)
        table = tab_ref[:, :, i * part : (i + 1) * part].reshape(128, part)
        acc[...] += jnp.dot(table, hot, preferred_element_type=F32)

    @pl.when(step == pl.num_programs(0) - 1)
    def _():
        u = lax.broadcasted_iota(jnp.int32, (ROWS, ROWS), 0)
        t = lax.broadcasted_iota(jnp.int32, (ROWS, ROWS), 1)
        tri = jnp.where(u <= t, 1.0, 0.0).astype(BF16)
        rate, raw = acc[0:64, :], acc[64:128, :]
        cum = jnp.dot(rate.astype(BF16), tri, preferred_element_type=F32) * (-LOG2E)
        size = jnp.maximum(raw, 0.0) + jnp.log1p(jnp.exp(-jnp.abs(raw)))
        both = jnp.concatenate([cum, cum - jnp.log(size) * LOG2E], 0)
        row_ref[...] = both
        col_ref[...] = both.T


def table_call(token_ids, token_tables):
    width = 4096
    return pl.pallas_call(
        table_kernel,
        out_shape=(
            jax.ShapeDtypeStruct((128, ROWS), F32),
            jax.ShapeDtypeStruct((ROWS, 128), F32),
        ),
        grid=(token_tables.shape[2] // width,),
        in_specs=[
            pl.BlockSpec((1, ROWS), lambda i: (0, 0)),
            pl.BlockSpec((2, 64, width), lambda i: (0, 0, i)),
        ],
        out_specs=[
            pl.BlockSpec((128, ROWS), lambda i: (0, 0)),
            pl.BlockSpec((ROWS, 128), lambda i: (0, 0)),
        ],
        scratch_shapes=[pltpu.VMEM((128, ROWS), F32)],
        compiler_params=params(),
        cost_estimate=cost(4e9, 2 * MIB),
        name="tables",
    )(token_ids.reshape(1, ROWS), token_tables)


def spread(values, first_head, width):
    hi, lo = split_hi_lo(values)
    r = lax.broadcasted_iota(jnp.int32, (64, width), 0)
    ch = lax.broadcasted_iota(jnp.int32, (64, width), 1)
    hot = jnp.where(r == first_head + ch // MHDIM, 1.0, 0.0).astype(BF16)
    return jnp.dot(
        jnp.concatenate([hi, lo], 1),
        jnp.concatenate([hot, hot], 0),
        preferred_element_type=F32,
    )


LANES = 128
STRIP = 64


def conv_strips(values_ref, front_ref, taps_ref, at, buffer, out_ref):
    buffer[0:16, :] = front_ref[:, at].astype(F32)
    for r in range(0, ROWS, STRIP):
        buffer[16 + r : 16 + r + STRIP, :] = values_ref[r : r + STRIP, at].astype(F32)
    taps = taps_ref[:, at].astype(F32)
    for r in range(0, ROWS, STRIP):
        total = taps[CONV - 1 : CONV] * buffer[16 + r : 16 + r + STRIP, :]
        for k in range(CONV - 1):
            total = total + taps[k : k + 1] * buffer[13 + k + r : 13 + k + r + STRIP, :]
        out_ref[r : r + STRIP, at] = silu(total).astype(BF16)


def state_kernel(group_ref, *refs):
    x_ref, xf_ref, xt_ref, b_ref, bf_ref, bt_ref, c_ref, cf_ref, ct_ref, col_ref = refs[:10]
    xc_ref, bc_ref, cc_ref, s_ref, buffer, scaled = refs[10:]
    group = group_ref[0]
    for i in range(STATE // LANES):
        at = slice(i * LANES, (i + 1) * LANES)
        conv_strips(b_ref, bf_ref, bt_ref, at, buffer.at[i], bc_ref)
        conv_strips(c_ref, cf_ref, ct_ref, at, buffer.at[2 + i], cc_ref)
    btrans = bc_ref[...].astype(F32).T.astype(BF16)
    last = col_ref[ROWS - 1 : ROWS, 0:64]
    tail = jnp.exp2(last - col_ref[:, 64:128])
    weights = jnp.concatenate([tail, jnp.broadcast_to(jnp.exp2(last), (EXTRA, 64))], 0)
    place = lax.broadcasted_iota(jnp.int32, (EXTRA, LANES), 0)
    for p in range(PAIRS):
        at = slice(p * LANES, (p + 1) * LANES)
        conv_strips(x_ref, xf_ref, xt_ref, at, buffer.at[p % 4], xc_ref)
        wide = spread(weights, group * 32 + 2 * p, LANES)
        for r in range(0, ROWS, STRIP):
            rows = slice(r, r + STRIP)
            scaled[p % 4, rows, :] = (xc_ref[rows, at].astype(F32) * wide[rows]).astype(BF16)
        state = jnp.dot(btrans, scaled[p % 4], preferred_element_type=F32)
        s_ref[p, 0:STATE, :] = state.astype(BF16)
        hi, lo = split_hi_lo(wide[ROWS:])
        edge = jnp.where(place == 0, hi.astype(F32), jnp.where(place == 1, lo.astype(F32), 0.0))
        s_ref[p, STATE:SROWS, :] = edge.astype(BF16)


def state_call(group, ssm_input, front, conv_input, bc, conv_bc, col):
    wide = lambda rows: pl.BlockSpec((rows, GROUP_CHANNELS), lambda j, g: (0, g[0]))
    narrow = lambda rows, base: pl.BlockSpec((rows, STATE), lambda j, g: (0, base + g[0]))
    whole = lambda shape: pl.BlockSpec(shape, lambda j, g: (0,) * len(shape))
    shapes = ((ROWS, GROUP_CHANNELS), (ROWS, STATE), (ROWS, STATE), (PAIRS, SROWS, 128))
    return pl.pallas_call(
        state_kernel,
        out_shape=tuple(jax.ShapeDtypeStruct(shape, BF16) for shape in shapes),
        grid_spec=pltpu.PrefetchScalarGridSpec(
            num_scalar_prefetch=1,
            grid=(1,),
            in_specs=[
                wide(ROWS),
                wide(16),
                wide(CONV),
                narrow(ROWS, 0),
                narrow(16, 16),
                narrow(CONV, 0),
                narrow(ROWS, 2),
                narrow(16, 18),
                narrow(CONV, 2),
                whole((ROWS, 128)),
            ],
            out_specs=[whole(shape) for shape in shapes],
            scratch_shapes=[
                pltpu.VMEM((4, 16 + ROWS, LANES), F32),
                pltpu.VMEM((4, ROWS, LANES), BF16),
            ],
        ),
        compiler_params=params(),
        cost_estimate=cost(4e9, 3 * MIB),
        name="conv_state",
    )(group, ssm_input, front, conv_input, bc, front, conv_bc, bc, front, conv_bc, col)


def inside_kernel(g_ref, x_ref, b_ref, c_ref, row_ref, col_ref, skip_ref, y_ref, gram, held):
    g = g_ref[0]
    half = ROWS // 2
    product = lax.dot_general(
        c_ref[...], b_ref[...], (((1,), (1,)), ((), ())), preferred_element_type=F32
    )
    t = lax.broadcasted_iota(jnp.int32, (ROWS, ROWS), 0)
    s = lax.broadcasted_iota(jnp.int32, (ROWS, ROWS), 1)
    gram[...] = jnp.where(s <= t, product, 0.0)
    columns = pltpu.roll(col_ref[...], lax.rem(128 - g * 32, 128), 1)
    lane = lax.broadcasted_iota(jnp.int32, (half, LANES), 1)
    for p in range(PAIRS):
        at = slice(p * LANES, (p + 1) * LANES)
        for i in range(2):
            h = 2 * p + i
            entries = row_ref[pl.ds(64 + g * 32 + h, 1), :]
            slot = held.at[2 * (p % 2) + i]
            for r in range(0, ROWS, STRIP):
                width = half if r < half else ROWS
                power = columns[r : r + STRIP, h : h + 1] - entries[:, :width]
                weight = gram[r : r + STRIP, :width] * jnp.exp2(jnp.minimum(power, 1.0))
                slot[r : r + STRIP, :width] = weight.astype(BF16)
        head = g * 32 + 2 * p
        skip = jnp.where(lane[0:1] < MHDIM, skip_ref[head], skip_ref[head + 1])
        for r, width in ((0, half), (half, ROWS)):
            first, second = (
                jnp.dot(
                    held[2 * (p % 2) + i, r : r + half, :width],
                    x_ref[:width, at],
                    preferred_element_type=F32,
                )
                for i in range(2)
            )
            rows = slice(r, r + half)
            y = jnp.where(lane < MHDIM, first, second) + skip * x_ref[rows, at].astype(F32)
            y_ref[rows, at] = y.astype(BF16)


def inside_call(group, x, b, c, row, col, skip):
    vmem = pl.BlockSpec(memory_space=pltpu.VMEM)
    smem = pl.BlockSpec(memory_space=pltpu.SMEM)
    return pl.pallas_call(
        inside_kernel,
        out_shape=jax.ShapeDtypeStruct((ROWS, GROUP_CHANNELS), BF16),
        in_specs=[smem, vmem, vmem, vmem, vmem, vmem, smem],
        out_specs=vmem,
        scratch_shapes=[pltpu.VMEM((ROWS, ROWS), F32), pltpu.VMEM((4, ROWS, ROWS), BF16)],
        compiler_params=params(),
        cost_estimate=cost(5e9, 3 * MIB),
        name="inside",
    )(group, x, b, c, row, col, skip)


def edge_of(s):
    return s[STATE : STATE + 1, :].astype(F32) + s[STATE + 1 : STATE + 2, :].astype(F32)


def combine_kernel(core_ref, own_ref, other_ref, out_ref):
    own_first = core_ref[0] == 0
    place = lax.broadcasted_iota(jnp.int32, (EXTRA, 128), 0)
    for p in range(PAIRS):
        own_edge, other_edge = edge_of(own_ref[p]), edge_of(other_ref[p])
        keep_own = jnp.where(own_first, other_edge, 1.0)
        keep_other = jnp.where(own_first, 1.0, own_edge)
        for r in range(0, STATE, STRIP):
            rows = slice(r, r + STRIP)
            own, other = own_ref[p, rows].astype(F32), other_ref[p, rows].astype(F32)
            out_ref[p, rows, :] = (keep_own * own + keep_other * other).astype(BF16)
        hi, lo = split_hi_lo(own_edge * other_edge)
        out_ref[p, STATE:SROWS, :] = jnp.where(
            place == 0, hi.astype(F32), jnp.where(place == 1, lo.astype(F32), 0.0)
        ).astype(BF16)


def combine_call(core, own, other):
    vmem = pl.BlockSpec(memory_space=pltpu.VMEM)
    return pl.pallas_call(
        combine_kernel,
        out_shape=jax.ShapeDtypeStruct((PAIRS, SROWS, 128), BF16),
        in_specs=[pl.BlockSpec(memory_space=pltpu.SMEM), vmem, vmem],
        out_specs=vmem,
        compiler_params=params(),
        cost_estimate=cost(2e9, 3 * MIB),
        name="combine",
    )(core, own, other)


def prefix_kernel(s_ref, out_ref):
    carried = jnp.zeros((STATE, 128), F32)
    for k in range(CHIPS):
        out_ref[k] = carried.astype(BF16)
        if k < CHIPS - 1:
            s = s_ref[k].astype(F32)
            carried = edge_of(s_ref[k]) * carried + s[:STATE]


def prefix_call(s):
    return pl.pallas_call(
        prefix_kernel,
        out_shape=jax.ShapeDtypeStruct((CHIPS, STATE, 128), BF16),
        in_specs=[pl.BlockSpec(memory_space=pltpu.VMEM)],
        out_specs=pl.BlockSpec(memory_space=pltpu.VMEM),
        compiler_params=params(),
        cost_estimate=cost(2e9, 2 * MIB),
        name="prefix",
    )(s)


def output_kernel(g_ref, s_ref, f_ref, c_ref, col_ref, y_ref, gate_ref, gain_ref, _, out_ref, held, state):
    group, core = g_ref[0], g_ref[1]

    @pl.when(pl.program_id(0) == 0)
    def _():
        for p in range(PAIRS):
            at = slice(p * LANES, (p + 1) * LANES)
            keep = jnp.where(core == 0, 1.0, edge_of(f_ref[p]))
            add = jnp.where(core == 0, 0.0, 1.0)
            for r in range(0, STATE, STRIP):
                rows = slice(r, r + STRIP)
                entering = keep * s_ref[p, rows].astype(F32) + add * f_ref[p, rows].astype(F32)
                state[rows, at] = entering.astype(BF16)

    rows = c_ref.shape[0]
    c = c_ref[...]
    grown = jnp.exp2(col_ref[:, 0:64])
    squares = jnp.zeros((rows, LANES), F32)
    for p in range(PAIRS):
        at = slice(p * LANES, (p + 1) * LANES)
        carried = jnp.dot(c, state[:, at], preferred_element_type=F32)
        factor = spread(grown, group * 32 + 2 * p, LANES)
        y = y_ref[:, at].astype(F32) + factor * carried
        gated = y * silu(gate_ref[:, at].astype(F32))
        squares = squares + gated * gated
        held[:, at] = gated
    mean = jnp.sum(squares, axis=1, keepdims=True) * (1.0 / GROUP_CHANNELS)
    scale = lax.rsqrt(mean + EPSILON)
    for p in range(PAIRS):
        at = slice(p * LANES, (p + 1) * LANES)
        out_ref[:, at] = (held[:, at] * scale * gain_ref[:, at].astype(F32)).astype(BF16)


def output_call(place, state, first, c, col, y, gate, gain, old):
    rows = 128
    whole = lambda n: pl.BlockSpec((PAIRS, n, 128), lambda i, g: (0, 0, 0))
    wide = pl.BlockSpec((rows, GROUP_CHANNELS), lambda i, g: (i, g[0]))
    in_specs = [
        whole(STATE),
        whole(SROWS),
        pl.BlockSpec((rows, STATE), lambda i, g: (i, 0)),
        pl.BlockSpec((rows, 128), lambda i, g: (i, 0)),
        pl.BlockSpec((rows, GROUP_CHANNELS), lambda i, g: (i, 0)),
        wide,
        pl.BlockSpec((1, GROUP_CHANNELS), lambda i, g: (0, g[0])),
    ]
    args = [place, state, first, c, col, y, gate, gain]
    if old is None:
        body = lambda *r: output_kernel(*r[:8], None, *r[8:])
        aliases = {}
    else:
        body = output_kernel
        in_specs.append(pl.BlockSpec(memory_space=pl.ANY))
        args.append(old)
        aliases = {8: 0}
    return pl.pallas_call(
        body,
        out_shape=jax.ShapeDtypeStruct((ROWS, 2 * GROUP_CHANNELS), BF16),
        grid_spec=pltpu.PrefetchScalarGridSpec(
            num_scalar_prefetch=1,
            grid=(ROWS // rows,),
            in_specs=in_specs,
            out_specs=wide,
            scratch_shapes=[
                pltpu.VMEM((rows, GROUP_CHANNELS), F32),
                pltpu.VMEM((STATE, GROUP_CHANNELS), BF16),
            ],
        ),
        input_output_aliases=aliases,
        compiler_params=params(),
        cost_estimate=cost(4e9, 5 * MIB),
        name="mixer_out",
    )(*args)


UNIT = 1024
SLOTS = 4
QPER = 8
SHARES = 6
SHARE_LANES = SLOTS * HDIM
SCALE = LOG2E * HDIM ** (-0.5)


GIVES = (14, 10)


def given(chip):
    return jnp.where(chip >= GIVES[0], 2, jnp.where(chip >= GIVES[1], 1, 0))


def attention_kernel(scal, own_ref, far_a, far_b, kv_hbm, out_ref, out_a, out_b, *scratch):
    kv, qs, acc, result, sem = scratch
    core, chip = scal[0], scal[1]
    cuts = sem.shape[0]
    length = kv.shape[0] // cuts
    copies = []
    for n in range(cuts):
        at = pl.ds(n * length, length)
        copies.append(pltpu.make_async_copy(kv_hbm.at[at], kv.at[at], sem.at[n]))
        copies[-1].start()
    for slot in range(SHARES * SLOTS):
        ref, h = own_ref, slot
        if slot >= 2 * QPER:
            ref, h = (far_a, far_b)[(slot - 2 * QPER) // SLOTS], slot % SLOTS
        hi, lo = split_hi_lo(ref[:, h * HDIM : (h + 1) * HDIM].astype(F32) * SCALE)
        qs[slot, :, 0:HDIM] = hi
        qs[slot, :, HDIM:] = lo
    for copy in copies:
        copy.wait()
    give, take = given(chip), given(CHIPS - 1 - chip)

    def share(j, carry):
        mirrored = j >= SHARES - 2
        its_chip = jnp.where(mirrored, CHIPS - 1 - chip, chip)
        its_core = jnp.where(mirrored, 1 - core, core)
        limit = its_chip // 2
        first_row = lax.rem(its_chip, 2) * (2 * ROWS) + its_core * ROWS
        used = jnp.where(
            j < 2, True, jnp.where(mirrored, take >= SHARES - j, give <= SHARES - 3 - j)
        )
        lane = jnp.where(j < 2, 0, HDIM)

        def scores_of(slot, keys):
            return lax.dot_general(
                qs[j * SLOTS + slot], keys, (((1,), (1,)), ((), ())), preferred_element_type=F32
            )

        def keys_values_of(u):
            rows = pl.ds(pl.multiple_of(u * UNIT, UNIT), UNIT)
            keys = kv[rows, pl.ds(pl.multiple_of(lane, HDIM), HDIM)]
            values = kv[rows, pl.ds(pl.multiple_of(2 * HDIM + lane, HDIM), HDIM)]
            keys = jnp.concatenate([keys, keys], 1)
            return keys, jnp.concatenate([values, jnp.ones((UNIT, HDIM), BF16)], 1)

        def visible_in(shift):
            row = lax.broadcasted_iota(jnp.int32, (ROWS, UNIT), 0) + first_row
            col = lax.broadcasted_iota(jnp.int32, (ROWS, UNIT), 1)
            return col + shift <= row

        def absorb(u, masked):
            keys, values = keys_values_of(u)
            scores = [scores_of(h, keys) for h in range(SLOTS)]
            for h in range(SLOTS):
                p = jnp.exp2(scores[h])
                if masked:
                    p = jnp.where(visible_in(0), p, 0.0)
                got = jnp.dot(p.astype(BF16), values, preferred_element_type=F32)
                acc[h] = got if masked else acc[h] + got

        @pl.when(used)
        def _():
            absorb(limit, True)

            def one(u, carry):
                absorb(u, False)
                return carry

            lax.fori_loop(0, limit, one, 0)
            least = jnp.full((ROWS, HDIM), 1.0, F32)
            most = jnp.full((ROWS, HDIM), 1.0, F32)
            for h in range(SLOTS):
                total = acc[h, :, HDIM:]
                least = jnp.minimum(least, total)
                most = jnp.maximum(most, total)
                result[j, :, h * HDIM : (h + 1) * HDIM] = (acc[h, :, :HDIM] / total).astype(BF16)
            safe = (jnp.min(least) > 2.0**-80) & (jnp.max(most) < 2.0**110)

            @pl.when(jnp.logical_not(safe))
            def _():
                def head(h, carry):
                    def unit_step(u, state):
                        top, total, summed = state
                        keys, values = keys_values_of(u)
                        shown = visible_in((u - limit) * UNIT)
                        scores = jnp.where(shown, scores_of(h, keys), -1e30)
                        new_top = jnp.maximum(top, jnp.max(scores, axis=1, keepdims=True))
                        shrink = jnp.exp2(top - new_top)
                        p = jnp.where(shown, jnp.exp2(scores - new_top), 0.0)
                        total = total * shrink + jnp.sum(p, axis=1, keepdims=True)
                        summed = summed * shrink + jnp.dot(
                            p.astype(BF16), values[:, :HDIM], preferred_element_type=F32
                        )
                        return new_top, total, summed

                    zero = jnp.zeros((ROWS, 1), F32)
                    state = (zero - 1e30, zero, jnp.zeros((ROWS, HDIM), F32))
                    _, total, summed = lax.fori_loop(0, limit + 1, unit_step, state)
                    at = pl.ds(pl.multiple_of(h * HDIM, HDIM), HDIM)
                    result[j, :, at] = (summed / total).astype(BF16)
                    return carry

                lax.fori_loop(0, SLOTS, head, 0)

        return carry

    lax.fori_loop(0, SHARES, share, 0)
    for j in range(SHARES):
        if j < SHARES - 2:
            out_ref[:, j * SHARE_LANES : (j + 1) * SHARE_LANES] = result[j]
    out_a[...] = result[SHARES - 2]
    out_b[...] = result[SHARES - 1]


def attention_call(scal, queries, far_a, far_b, kv):
    vmem = pl.BlockSpec(memory_space=pltpu.VMEM)
    return pl.pallas_call(
        attention_kernel,
        out_shape=(
            jax.ShapeDtypeStruct((ROWS, 2 * QPER * HDIM), BF16),
            jax.ShapeDtypeStruct((ROWS, SHARE_LANES), BF16),
            jax.ShapeDtypeStruct((ROWS, SHARE_LANES), BF16),
        ),
        in_specs=[
            pl.BlockSpec(memory_space=pltpu.SMEM),
            vmem,
            vmem,
            vmem,
            pl.BlockSpec(memory_space=pl.ANY),
        ],
        out_specs=(vmem, vmem, vmem),
        scratch_shapes=[
            pltpu.VMEM(kv.shape, BF16),
            pltpu.VMEM((SHARES * SLOTS, ROWS, 2 * HDIM), BF16),
            pltpu.VMEM((SLOTS, ROWS, 2 * HDIM), F32),
            pltpu.VMEM((SHARES, ROWS, SHARE_LANES), BF16),
            pltpu.SemaphoreType.DMA((4,)),
        ],
        compiler_params=params(32),
        cost_estimate=cost(3.2e10, 12 * MIB),
        name="attention",
    )(scal, queries, far_a, far_b, kv)


def permute(value, target):
    pairs = []
    for place in range(NY * NX * NCORE):
        y, x, c = place // (NX * NCORE), (place // NCORE) % NX, place % NCORE
        y, x, c = target(y, x, c)
        pairs.append((place, ((y % NY) * NX + x % NX) * NCORE + c))
    return lax.ppermute(value, "seq", pairs)


def swap(value):
    return permute(value, lambda y, x, c: (y, x, 1 - c))


ALL_CHIPS = [[chip * NCORE + core for chip in range(CHIPS)] for core in range(NCORE)]


def exchange(value):
    return lax.all_to_all(value, "seq", 0, 0, axis_index_groups=ALL_CHIPS, tiled=True)


def mirror(value, first_chip, to_low):
    seq = CHIPS * NCORE
    pairs = [(place, seq - 1 - place) for place in range(first_chip * NCORE, seq)]
    return lax.ppermute(value, "seq", pairs if to_low else [(low, high) for high, low in pairs])


def local(
    token_ids,
    token_tables,
    ssm_input,
    ssm_gate,
    ssm_bc,
    conv_input,
    conv_bc,
    skip_gain,
    norm_gain,
    queries,
    keys_values,
):
    place = lax.axis_index("seq")
    core = lax.rem(place, NCORE)
    chip = place // NCORE
    keep = core.reshape(1)

    kv = lax.all_gather(keys_values.reshape(ROWS, -1), "seq", axis=0, tiled=True)

    bc = ssm_bc.reshape(ROWS, -1)
    edge = jnp.concatenate([ssm_input[ROWS - 16 :], bc[ROWS - 16 :]], 1)
    seq = NY * NX * NCORE
    front = lax.ppermute(edge, "seq", [(i, i + 1) for i in range(seq - 1)])

    scal = jnp.stack([core, chip]).astype(jnp.int32)
    half = QPER * HDIM
    quarter = SHARE_LANES
    far_b = mirror(queries[:, half + quarter :], GIVES[1], True)
    far_a = mirror(queries[:, half : half + quarter], GIVES[0], True)

    row, col = table_call(token_ids, token_tables)
    taps_bc = conv_bc.reshape(CONV, -1)
    send = 1 - keep
    x_s, b_s, c_s, state_s = state_call(send, ssm_input, front, conv_input, bc, taps_bc, col)
    state_o = swap(state_s)
    col_k, far_b, far_a = lax.optimization_barrier((col, far_b, far_a))
    x_k, b_k, c_k, state_k = state_call(keep, ssm_input, front, conv_input, bc, taps_bc, col_k)
    joined = combine_call(keep, state_k, state_o)
    arrived = exchange(joined)
    y_s = inside_call(send, x_s, b_s, c_s, row, col, skip_gain)
    y_k = inside_call(keep, x_k, b_k, c_k, row, col, skip_gain)
    first_s = swap(state_k)
    arrived, y_k, y_s, first_s = lax.optimization_barrier((arrived, y_k, y_s, first_s))
    before = prefix_call(arrived)
    scal, before = lax.optimization_barrier((scal, before))
    entering_k = exchange(before)
    own, out_a, out_b = attention_call(scal, queries, far_a, far_b, kv)
    y_k, y_s, out_a, out_b, entering_k = lax.optimization_barrier(
        (y_k, y_s, out_a, out_b, entering_k)
    )
    entering_s = swap(entering_k)
    back_b, back_a = mirror(out_b, GIVES[1], False), mirror(out_a, GIVES[0], False)

    gain = norm_gain.reshape(1, -1)
    place_k = jnp.stack([core, core]).astype(jnp.int32)
    place_s = jnp.stack([1 - core, core]).astype(jnp.int32)
    mixed = output_call(place_k, entering_k, state_o, c_k, col, y_k, ssm_gate, gain, None)
    mixed = output_call(place_s, entering_s, first_s, c_s, col, y_s, ssm_gate, gain, mixed)
    give = given(chip)
    mixed, back_a, back_b = lax.optimization_barrier((mixed, back_a, back_b))
    attn = jnp.concatenate(
        [
            own[:, :half],
            jnp.where(give >= 2, back_a, own[:, half : half + quarter]),
            jnp.where(give >= 1, back_b, own[:, half + quarter :]),
        ],
        1,
    )
    return mixed, attn


def solution(mesh):
    in_specs = (
        P(("dp", "seq")),
        P(None, "head", None),
        P(("dp", "seq"), "head"),
        P(("dp", "seq"), "head"),
        P(("dp", "seq"), None, "head"),
        P(None, "head"),
        P(None, None, "head"),
        P("head"),
        P("head"),
        P(("dp", "seq"), "head"),
        P(("dp", "seq"), None, "head"),
    )
    out_specs = (P(("dp", "seq"), "head"), P(("dp", "seq"), "head"))
    return jax.shard_map(local, mesh=mesh, in_specs=in_specs, out_specs=out_specs, check_vma=False)
```

time: 870 us -> 179 us (0.21)
  the two profiles are of different devices: /device:TPU:95 before, /device:TPU:33 now
where the time goes in v1:
time: 179 us; the launch traced here: 177 us
  Pallas kernels  87.6 us (49%)
  local copies, waits for them, and re-layouts  29.8 us (17%)
  waiting for transfers between devices  27.2 us (15%)
  starting transfers between devices  17.1 us (10%)
  between operations  14.4 us (8%)
    pallas_call x1, Pallas kernels, attention_call(): pl.pallas_call(attention_kernel, out_shape=(jax.ShapeDtypeStruct((ROWS, 2...  55.5 us
    unnamed x88, local copies, waits for them, and re-layouts  27.1 us
    ppermute x4, waiting for transfers between devices, mirror(): lax.ppermute(value, 'seq', pairs if to_low else [(low, high) for high, lo...  17.2 us
    pallas_call x2, Pallas kernels, state_call(): pl.pallas_call(state_kernel, out_shape=tuple((jax.ShapeDtypeStruct(shape,...  12.3 us
    all_to_all x2, waiting for transfers between devices, exchange(): lax.all_to_all(value, 'seq', 0, 0, axis_index_groups=ALL_CHIPS, tiled=True)  10 us
    pallas_call x2, Pallas kernels, output_call(): pl.pallas_call(body, out_shape=jax.ShapeDtypeStruct((ROWS, 2 * GROUP_CHAN...  8.63 us
    all_to_all x2, starting transfers between devices, exchange(): lax.all_to_all(value, 'seq', 0, 0, axis_index_groups=ALL_CHIPS, tiled=True)  7.68 us
    pallas_call x2, Pallas kernels, inside_call(): pl.pallas_call(inside_kernel, out_shape=jax.ShapeDtypeStruct((ROWS, GROUP...  5.43 us
  transfers between devices with their start and end apart: 11, of which 3 were waited for; matrix products, arithmetic and copies ran while one was open for 2% of the time, Pallas kernels for 49%

profile of v1, /device:TPU:33, one launch (start us, length us, event | category | flops | bytes accessed | tf_op | source)
XLA Modules:
  0.0 177.5 jit_solution(17492934711641176166)
XLA Ops:
  7.2 0.0 all-gather.2.cloned.1.call-start
  7.2 1.7 copy.17
  8.9 0.0 all-gather.2.cloned.1.call-update
  8.9 0.9 slice.24
  9.8 0.8 slice.25
  10.7 3.7 %collective-permute-start = (bf16[16,5120]{1,0:T(8,128)(2,1)S(1)}, bf16[16,5120]{1,0:T(8,128)(2,1)S(1)}, u32[]{:S(2)}, u32[]{:S(2)}) collective-permute-start(bf16[16,5120]{1,0:T(8,128)(2,1)S(1)} %pad_maximum_fusion.1), channel_id=1, source_target_pairs={{0,4},{4,8},{8,12},{12,16},{16,20},{20,24},{24,28},{28,32},{32,36}... | collective-permute-start | bytes 491528 | tf_op jit(solution)/shard_map/ppermute | solution.py:580
  14.4 0.0 copy-start.4
  14.4 1.6 copy-done.4
  16.0 0.7 copy-done.14
  16.6 1.4 tables.1
  18.0 0.1 copy.15
  18.1 0.0 collective-permute-done.refs_1_.refs_4_.refs_7_
  18.2 0.5 copy-done.37
  18.7 1.6 copy-done.1
  20.3 6.2 %conv_state.3 = (bf16[256,2048]{1,0:T(8,128)(2,1)S(1)}, bf16[256,256]{1,0:T(8,128)(2,1)S(1)}, bf16[256,256]{1,0:T(8,128)(2,1)S(1)}, bf16[16,272,128]{2,1,0:T(8,128)(2,1)}) custom-call(s32[1]{0:T(128)S(6)} %sub.11.group_ref.g_ref, bf16[256,4096]{1,0:T(8,128)(2,1)S(1)} %copy-done.1, bf16[16,5120]{1,0:T(8,128)(2,1)S(1)} %collective-permute-done.refs_1_.refs_4_.refs_7_, ...), custom_call_target="tpu_custom_call" | custom-call | flops 4000000000 | bytes 3145728 | tf_op jit(solution)/shard_map/conv_state/pallas_call | solution.py:160
  26.4 0.6 copy-done.27
  27.1 0.7 copy-done.33
  27.7 0.9 fusion
  28.7 1.3 collective-permute-start.1
  30.0 1.3 collective-permute-start.2
  31.3 11.6 %collective-permute-done.1.far_b = bf16[256,512]{1,0:T(8,128)(2,1)S(1)} collective-permute-done((bf16[256,512]{1,0:T(8,128)(2,1)}, bf16[256,512]{1,0:T(8,128)(2,1)S(1)}, u32[]{:S(2)}, u32[]{:S(2)}) %collective-permute-start.1) | collective-permute-done | bytes 262176 | tf_op jit(solution)/shard_map/ppermute | solution.py:554
  42.9 5.5 %collective-permute-done.2.far_a = bf16[256,512]{1,0:T(8,128)(2,1)S(1)} collective-permute-done((bf16[256,512]{1,0:T(8,128)(2,1)}, bf16[256,512]{1,0:T(8,128)(2,1)S(1)}, u32[]{:S(2)}, u32[]{:S(2)}) %collective-permute-start.2) | collective-permute-done | bytes 262176 | tf_op jit(solution)/shard_map/ppermute | solution.py:554
  48.5 1.6 copy-done.2
  50.1 0.9 copy-done.25
  51.0 6.2 %conv_state.2 = (bf16[256,2048]{1,0:T(8,128)(2,1)S(1)}, bf16[256,256]{1,0:T(8,128)(2,1)S(1)}, bf16[256,256]{1,0:T(8,128)(2,1)S(1)}, bf16[16,272,128]{2,1,0:T(8,128)(2,1)}) custom-call(s32[1]{0:T(128)} %bitcast.1.group_ref.core_ref.g_ref, bf16[256,4096]{1,0:T(8,128)(2,1)S(1)} %copy-done.2, bf16[16,5120]{1,0:T(8,128)(2,1)S(1)} %collective-permute-done.refs_1_.refs_4_.refs_7_, ...), custom_call_target="tpu_custom_call" | custom-call | flops 4000000000 | bytes 3145728 | tf_op jit(solution)/shard_map/conv_state/pallas_call | solution.py:160
  57.1 1.0 copy-done.22
  58.1 0.7 copy-done.30
  58.8 0.7 copy-done.35
  59.4 0.5 collective-permute-start.4
  59.9 0.0 collective-permute-done.3.other_ref.r_2_
  59.9 3.1 %combine.1 = bf16[16,272,128]{2,1,0:T(8,128)(2,1)} custom-call(s32[1]{0:T(128)} %bitcast.1.group_ref.core_ref.g_ref, bf16[16,272,128]{2,1,0:T(8,128)(2,1)} %get-tuple-element.34.own_ref, bf16[16,272,128]{2,1,0:T(8,128)(2,1)S(1)} %collective-permute-done.3.other_ref.r_2_), custom_call_target="tpu_custom_call" | custom-call | flops 2000000000 | bytes 3145728 | tf_op jit(solution)/shard_map/combine/pallas_call | solution.py:266
  63.1 4.0 %all-to-all-start = ((bf16[16,272,128]{2,1,0:T(8,128)(2,1)}), bf16[16,272,128]{2,1,0:T(8,128)(2,1)S(1)}, u32[]{:S(2)}, u32[]{:S(2)}) async-start(bf16[16,272,128]{2,1,0:T(8,128)(2,1)} %combine.1), calls=%async_computation | async-start | bytes 2228224 | tf_op jit(solution)/shard_map/all_to_all | solution.py:548
  67.1 0.1 pad_add_fusion.1.scal
  67.2 0.0 copy-start.21
  67.2 1.2 copy-done.21
  68.4 0.9 copy-done.38
  69.3 2.7 %inside.3.y_ref = bf16[256,2048]{1,0:T(8,128)(2,1)S(1)} custom-call(s32[1]{0:T(128)S(6)} %sub.11.group_ref.g_ref, bf16[256,2048]{1,0:T(8,128)(2,1)S(1)} %copy-done.21, bf16[256,256]{1,0:T(8,128)(2,1)S(1)} %copy-done.34, bf16[256,256]{1,0:T(8,128)(2,1)S(1)} %copy-done.28, f32[128,256]{1,0:T(8,128)S(1)} %copy-done.38, f32[256,128]{1,0:T(8,128)S(1)} %copy-done.26, ...), custom_call_target="tpu_custom_call" | custom-call | flops 5000000000 | bytes 3145728 | tf_op jit(solution)/shard_map/inside/pallas_call | solution.py:231
  72.1 1.0 copy-done.16
  73.1 2.7 %inside.2.r_5_ = bf16[256,2048]{1,0:T(8,128)(2,1)S(1)} custom-call(s32[1]{0:T(128)} %bitcast.1.group_ref.core_ref.g_ref, bf16[256,2048]{1,0:T(8,128)(2,1)S(1)} %copy-done.23, bf16[256,256]{1,0:T(8,128)(2,1)S(1)} %copy-done.36, bf16[256,256]{1,0:T(8,128)(2,1)S(1)} %copy-done.31, f32[128,256]{1,0:T(8,128)S(1)} %copy-done.38, f32[256,128]{1,0:T(8,128)S(1)} %copy-done.26, ...), custom_call_target="tpu_custom_call" | custom-call | flops 5000000000 | bytes 3145728 | tf_op jit(solution)/shard_map/inside/pallas_call | solution.py:231
  75.8 1.0 copy-done.18
  76.8 10.0 %all-to-all-done.s_ref = bf16[16,272,128]{2,1,0:T(8,128)(2,1)S(1)} async-done(((bf16[16,272,128]{2,1,0:T(8,128)(2,1)}), bf16[16,272,128]{2,1,0:T(8,128)(2,1)S(1)}, u32[]{:S(2)}, u32[]{:S(2)}) %all-to-all-start) | async-done | bytes 1114144 | tf_op jit(solution)/shard_map/all_to_all | solution.py:548
  86.8 1.2 prefix.1
  88.0 3.7 %all-to-all-start.1 = ((bf16[16,256,128]{2,1,0:T(8,128)(2,1)}), bf16[16,256,128]{2,1,0:T(8,128)(2,1)S(1)}, u32[]{:S(2)}, u32[]{:S(2)}) async-start(bf16[16,256,128]{2,1,0:T(8,128)(2,1)} %prefix.1), calls=%async_computation.1 | async-start | bytes 2097152 | tf_op jit(solution)/shard_map/all_to_all | solution.py:548
  91.7 0.0 all-gather.2.cloned.1.call-done.kv_hbm
  91.7 3.4 %copy-done.3 = bf16[8192,512]{1,0:T(8,128)(2,1)S(1)} copy-done((bf16[8192,512]{1,0:T(8,128)(2,1)S(1)}, bf16[8192,512]{1,0:T(8,128)(2,1)}, u32[]{:S(2)}) %copy-start.3) | copy-done | bytes 8388632
  95.1 0.9 copy-done.10
  96.1 55.5 %attention.1 = (bf16[256,2048]{1,0:T(8,128)(2,1)S(1)}, bf16[256,512]{1,0:T(8,128)(2,1)S(1)}, bf16[256,512]{1,0:T(8,128)(2,1)S(1)}) custom-call(s32[2]{0:T(128)S(1)} %pad_add_fusion.1.scal, bf16[256,2048]{1,0:T(8,128)(2,1)S(1)} %copy-done, bf16[256,512]{1,0:T(8,128)(2,1)S(1)} %copy-done.10, bf16[256,512]{1,0:T(8,128)(2,1)S(1)} %collective-permute-done.1.far_b, ...), custom_call_target="tpu_custom_call" | custom-call | flops 32000000000 | bytes 12582912 | tf_op jit(solution)/shard_map/attention/pallas_call | solution.py:503
  151.6 0.7 copy-done.11
  152.3 0.7 copy-done.12
  153.0 0.0 all-to-all-done.1.r_1_
  153.0 0.0 collective-permute-start.5
  153.0 0.1 pad_add_fusion.2.r_0_
  153.1 0.1 pad_add_fusion.g_ref
  153.2 1.3 collective-permute-start.6
  154.5 1.3 collective-permute-start.7
  155.9 0.0 copy-start.5
  155.9 1.6 copy-done.5
  157.5 1.2 copy-done.8
  158.7 1.2 copy-done.19
  159.9 0.9 copy-done.32
  160.8 3.7 %mixer_out.2._ = bf16[256,4096]{1,0:T(8,128)(2,1)} custom-call(s32[2]{0:T(128)S(1)} %pad_add_fusion.2.r_0_, bf16[16,256,128]{2,1,0:T(8,128)(2,1)S(1)} %all-to-all-done.1.r_1_, bf16[16,272,128]{2,1,0:T(8,128)(2,1)S(1)} %copy-done.8, bf16[256,256]{1,0:T(8,128)(2,1)S(1)} %copy-done.32, f32[256,128]{1,0:T(8,128)S(1)} %copy-done.26, ...), custom_call_target="tpu_custom_call" | custom-call | flops 4000000000 | bytes 5242880 | tf_op jit(solution)/shard_map/mixer_out/pallas_call | solution.py:353
  164.6 4.9 %mixer_out.3 = bf16[256,4096]{1,0:T(8,128)(2,1)} custom-call(s32[2]{0:T(128)S(1)} %pad_add_fusion.g_ref, bf16[16,256,128]{2,1,0:T(8,128)(2,1)S(1)} %collective-permute-done.5.s_ref, bf16[16,272,128]{2,1,0:T(8,128)(2,1)} %collective-permute-done.4.f_ref, bf16[256,256]{1,0:T(8,128)(2,1)S(1)} %copy-done.29, ...), custom_call_target="tpu_custom_call", output_to_operand_aliasing={{}: (8, {})} | custom-call | flops 4000000000 | bytes 5242880 | tf_op jit(solution)/shard_map/mixer_out/pallas_call | solution.py:353
  169.5 0.1 slice_select_fusion.1
  169.6 1.1 pad_maximum_fusion
  (68 shorter events, 0.2 us)
Async XLA Ops:
  7.2 84.5 %all-gather.2.cloned.1.call-start = ((), (), s32[]{:S(2)}) async-start(), calls=%async_computation.2 | async-start | bytes 8650752 | tf_op jit(solution)/shard_map/all_gather | solution.py:575
  10.7 7.5 %collective-permute-start = (bf16[16,5120]{1,0:T(8,128)(2,1)S(1)}, bf16[16,5120]{1,0:T(8,128)(2,1)S(1)}, u32[]{:S(2)}, u32[]{:S(2)}) collective-permute-start(bf16[16,5120]{1,0:T(8,128)(2,1)S(1)} %pad_maximum_fusion.1), channel_id=1, source_target_pairs={{0,4},{4,8},{8,12},{12,16},{16,20},{20,24},{24,28},{28,32},{32,36}... | collective-permute-start | bytes 491528 | tf_op jit(solution)/shard_map/ppermute | solution.py:580
  14.4 1.6 copy-start.4
  16.0 0.7 copy-start.14
  16.6 1.4 copy-start.39
  16.6 1.5 copy-start.41
  16.6 2.0 %copy-start.13 = (bf16[4,4096]{1,0:T(4,128)(2,1)S(1)}, bf16[4,4096]{1,0:T(4,128)(2,1)}, u32[]{:S(2)}) copy-start(bf16[4,4096]{1,0:T(4,128)(2,1)} %refs_2_.3) | copy-start | bytes 98308
  18.0 0.7 copy-start.37
  18.0 8.4 %copy-start.24 = (f32[256,128]{1,0:T(8,128)}, f32[256,128]{1,0:T(8,128)S(1)}, u32[]{:S(2)}) copy-start(f32[256,128]{1,0:T(8,128)S(1)} %get-tuple-element.33.refs_9_.col_ref.r_4_) | copy-start | bytes 393220
  18.7 1.6 copy-start.1
  20.3 7.5 %copy-start = (bf16[256,2048]{1,0:T(8,128)(2,1)S(1)}, bf16[256,2048]{1,0:T(8,128)(2,1)}, u32[]{:S(2)}) copy-start(bf16[256,2048]{1,0:T(8,128)(2,1)} %own_ref.1) | copy-start | bytes 3145732
  26.4 0.7 copy-start.27
  27.1 0.7 copy-start.33
  27.7 2.2 %copy-start.20 = (bf16[256,2048]{1,0:T(8,128)(2,1)}, bf16[256,2048]{1,0:T(8,128)(2,1)S(1)}, u32[]{:S(2)}) copy-start(bf16[256,2048]{1,0:T(8,128)(2,1)S(1)} %get-tuple-element.40.x_ref) | copy-start | bytes 3145732
  27.7 32.2 %collective-permute-start.3 = (bf16[16,272,128]{2,1,0:T(8,128)(2,1)}, bf16[16,272,128]{2,1,0:T(8,128)(2,1)S(1)}, u32[]{:S(2)}, u32[]{:S(2)}) collective-permute-start(bf16[16,272,128]{2,1,0:T(8,128)(2,1)} %get-tuple-element.35), channel_id=1, source_target_pairs={{0,4},{4,0},{8,12},{12,8},{16,20},{20,16},{24,28},{28,24},{32,36},... | collective-permute-start | bytes 3342344 | tf_op jit(solution)/shard_map/ppermute | solution.py:537
  28.7 14.3 %collective-permute-start.1 = (bf16[256,512]{1,0:T(8,128)(2,1)}, bf16[256,512]{1,0:T(8,128)(2,1)S(1)}, u32[]{:S(2)}, u32[]{:S(2)}) collective-permute-start(bf16[256,512]{1,0:T(8,128)(2,1)} %get-tuple-element.65), channel_id=1, source_target_pairs={{80,44},{84,40},{88,36},{92,32},{96,28},{100,24},{104,20},{108,16}... | collective-permute-start | bytes 786440 | tf_op jit(solution)/shard_map/ppermute | solution.py:554
  30.0 18.5 %collective-permute-start.2 = (bf16[256,512]{1,0:T(8,128)(2,1)}, bf16[256,512]{1,0:T(8,128)(2,1)S(1)}, u32[]{:S(2)}, u32[]{:S(2)}) collective-permute-start(bf16[256,512]{1,0:T(8,128)(2,1)} %get-tuple-element.64), channel_id=1, source_target_pairs={{112,12},{116,8},{120,4},{124,0},{113,13},{117,9},{121,5},{125,1},... | collective-permute-start | bytes 786440 | tf_op jit(solution)/shard_map/ppermute | solution.py:554
  48.5 1.6 copy-start.2
  50.1 0.9 copy-start.25
  51.0 6.2 %copy-start.9 = (bf16[256,512]{1,0:T(8,128)(2,1)}, bf16[256,512]{1,0:T(8,128)(2,1)S(1)}, u32[]{:S(2)}) copy-start(bf16[256,512]{1,0:T(8,128)(2,1)S(1)} %collective-permute-done.2.far_a) | copy-start | bytes 786436
  57.1 1.0 copy-start.22
  58.1 0.7 copy-start.30
  58.8 0.7 copy-start.35
  59.4 17.4 %collective-permute-start.4 = (bf16[16,272,128]{2,1,0:T(8,128)(2,1)}, bf16[16,272,128]{2,1,0:T(8,128)(2,1)}, u32[]{:S(2)}, u32[]{:S(2)}) collective-permute-start(bf16[16,272,128]{2,1,0:T(8,128)(2,1)} %get-tuple-element.34.own_ref), channel_id=1, source_target_pairs={{0,4},{4,0},{8,12},{12,8},{16,20},{20,16},{24,28},{28,24},{32,36},... | collective-permute-start | bytes 3342344 | tf_op jit(solution)/shard_map/ppermute | solution.py:537
  59.9 3.1 %copy-start.7 = (bf16[16,272,128]{2,1,0:T(8,128)(2,1)}, bf16[16,272,128]{2,1,0:T(8,128)(2,1)S(1)}, u32[]{:S(2)}) copy-start(bf16[16,272,128]{2,1,0:T(8,128)(2,1)S(1)} %collective-permute-done.3.other_ref.r_2_) | copy-start | bytes 3342340
  63.0 4.1 %copy-start.15 = (f32[64]{0:T(128)S(1)}, f32[64]{0:T(128)}, u32[]{:S(2)}) copy-start(f32[64]{0:T(128)} %skip_ref.3) | copy-start | bytes 772
  63.1 4.1 %copy-start.26 = (f32[256,128]{1,0:T(8,128)S(1)}, f32[256,128]{1,0:T(8,128)}, u32[]{:S(2)}) copy-start(f32[256,128]{1,0:T(8,128)} %copy-done.24) | copy-start | bytes 393220
  63.1 4.1 %copy-start.28 = (bf16[256,256]{1,0:T(8,128)(2,1)S(1)}, bf16[256,256]{1,0:T(8,128)(2,1)}, u32[]{:S(2)}) copy-start(bf16[256,256]{1,0:T(8,128)(2,1)} %copy-done.27) | copy-start | bytes 393220
  63.1 4.1 %copy-start.34 = (bf16[256,256]{1,0:T(8,128)(2,1)S(1)}, bf16[256,256]{1,0:T(8,128)(2,1)}, u32[]{:S(2)}) copy-start(bf16[256,256]{1,0:T(8,128)(2,1)} %copy-done.33) | copy-start | bytes 393220
  63.1 23.8 %all-to-all-start = ((bf16[16,272,128]{2,1,0:T(8,128)(2,1)}), bf16[16,272,128]{2,1,0:T(8,128)(2,1)S(1)}, u32[]{:S(2)}, u32[]{:S(2)}) async-start(bf16[16,272,128]{2,1,0:T(8,128)(2,1)} %combine.1), calls=%async_computation | async-start | bytes 2228224 | tf_op jit(solution)/shard_map/all_to_all | solution.py:548
  67.2 1.2 copy-start.21
  68.4 0.9 copy-start.38
  69.3 3.8 %copy-start.23 = (bf16[256,2048]{1,0:T(8,128)(2,1)S(1)}, bf16[256,2048]{1,0:T(8,128)(2,1)}, u32[]{:S(2)}) copy-start(bf16[256,2048]{1,0:T(8,128)(2,1)} %copy-done.22) | copy-start | bytes 3145732
  69.3 3.8 %copy-start.31 = (bf16[256,256]{1,0:T(8,128)(2,1)S(1)}, bf16[256,256]{1,0:T(8,128)(2,1)}, u32[]{:S(2)}) copy-start(bf16[256,256]{1,0:T(8,128)(2,1)} %copy-done.30) | copy-start | bytes 393220
  69.3 3.8 %copy-start.36 = (bf16[256,256]{1,0:T(8,128)(2,1)S(1)}, bf16[256,256]{1,0:T(8,128)(2,1)}, u32[]{:S(2)}) copy-start(bf16[256,256]{1,0:T(8,128)(2,1)} %copy-done.35) | copy-start | bytes 393220
  72.0 1.1 copy-start.16
  75.8 1.0 copy-start.18
  88.0 65.0 %all-to-all-start.1 = ((bf16[16,256,128]{2,1,0:T(8,128)(2,1)}), bf16[16,256,128]{2,1,0:T(8,128)(2,1)S(1)}, u32[]{:S(2)}, u32[]{:S(2)}) async-start(bf16[16,256,128]{2,1,0:T(8,128)(2,1)} %prefix.1), calls=%async_computation.1 | async-start | bytes 2097152 | tf_op jit(solution)/shard_map/all_to_all | solution.py:548
  91.7 3.4 %copy-start.3 = (bf16[8192,512]{1,0:T(8,128)(2,1)S(1)}, bf16[8192,512]{1,0:T(8,128)(2,1)}, u32[]{:S(2)}) copy-start(bf16[8192,512]{1,0:T(8,128)(2,1)} %all-gather.2.cloned.1.call-done.kv_hbm) | copy-start | bytes 25165828
  95.1 0.9 copy-start.10
  96.1 57.0 %copy-start.40 = (bf16[4096]{0:T(1024)(128)(2,1)S(1)}, bf16[4096]{0:T(1024)(128)(2,1)}, u32[]{:S(2)}) copy-start(bf16[4096]{0:T(1024)(128)(2,1)} %param.19) | copy-start | bytes 24580
  151.6 0.7 copy-start.11
  152.3 0.7 copy-start.12
  153.0 11.5 %collective-permute-start.5 = (bf16[16,256,128]{2,1,0:T(8,128)(2,1)S(1)}, bf16[16,256,128]{2,1,0:T(8,128)(2,1)S(1)}, u32[]{:S(2)}, u32[]{:S(2)}) collective-permute-start(bf16[16,256,128]{2,1,0:T(8,128)(2,1)S(1)} %all-to-all-done.1.r_1_), channel_id=1, source_target_pairs={{0,4},{4,0},{8,12},{12,8},{16,20},{20,16},{24,28},{28,24},{32,36},... | collective-permute-start | bytes 3145736 | tf_op jit(solution)/shard_map/ppermute | solution.py:537
  153.2 16.3 %collective-permute-start.6 = (bf16[256,512]{1,0:T(8,128)(2,1)}, bf16[256,512]{1,0:T(8,128)(2,1)S(1)}, u32[]{:S(2)}, u32[]{:S(2)}) collective-permute-start(bf16[256,512]{1,0:T(8,128)(2,1)} %copy-done.12), channel_id=1, source_target_pairs={{12,112},{8,116},{4,120},{0,124},{13,113},{9,117},{5,121},{1,125},... | collective-permute-start | bytes 786440 | tf_op jit(solution)/shard_map/ppermute | solution.py:554
  154.5 15.0 %collective-permute-start.7 = (bf16[256,512]{1,0:T(8,128)(2,1)}, bf16[256,512]{1,0:T(8,128)(2,1)S(1)}, u32[]{:S(2)}, u32[]{:S(2)}) collective-permute-start(bf16[256,512]{1,0:T(8,128)(2,1)} %copy-done.11), channel_id=1, source_target_pairs={{44,80},{40,84},{36,88},{32,92},{28,96},{24,100},{20,104},{16,108}... | collective-permute-start | bytes 786440 | tf_op jit(solution)/shard_map/ppermute | solution.py:554
  155.9 1.6 copy-start.5
  157.4 1.2 copy-start.8
  158.7 1.2 copy-start.19
  159.9 0.9 copy-start.32
  160.8 3.7 %copy-start.6 = (bf16[256,4096]{1,0:T(8,128)(2,1)S(1)}, bf16[256,4096]{1,0:T(8,128)(2,1)}, u32[]{:S(2)}) copy-start(bf16[256,4096]{1,0:T(8,128)(2,1)} %gate_ref.1) | copy-start | bytes 6291460
  160.8 3.7 %copy-start.17 = (bf16[256,2048]{1,0:T(8,128)(2,1)S(1)}, bf16[256,2048]{1,0:T(8,128)(2,1)}, u32[]{:S(2)}) copy-start(bf16[256,2048]{1,0:T(8,128)(2,1)} %copy-done.16) | copy-start | bytes 3145732
  160.8 3.7 %copy-start.29 = (bf16[256,256]{1,0:T(8,128)(2,1)S(1)}, bf16[256,256]{1,0:T(8,128)(2,1)}, u32[]{:S(2)}) copy-start(bf16[256,256]{1,0:T(8,128)(2,1)} %copy-done.27) | copy-start | bytes 393220
Sparse Core Ops, SparseCore 0:
  10.3 57.0 all-gather.1
